TPU v7x, 512 devices: a whole 4x8x8 slice. The times are simulated.
512 devices in a mesh: group: 4 (over x), seq: 128 (over z, y, core).
Axes of the slice: x: 4, y: 8, z: 8, core: 2. Of those that a mesh axis runs over, the one named last changes fastest.
Arguments:
- query_vectors: bfloat16 [4, 3072, 4096], P('group', 'seq'), may hold values from -5 to 5
- key_vectors: bfloat16 [4, 3072, 4096], P('group', 'seq'), may hold values from -5 to 5
- value_vectors: bfloat16 [4, 3072, 4096], P('group', 'seq'), may hold values from -6 to 6
- levels: int32 [4], replicated, may hold values from 0 to 49
- causal_order: int32 [4], replicated, may hold values from 0 to 3999, as said below
- level_gates: float32 [50, 4096], replicated, may hold values from 0.25 to 2
Outputs:
- gated_attention: bfloat16 [4, 3072, 4096], P('group', 'seq')
Inputs may be any that keep to these rules, and one draw needn't show every extreme that they name: `causal_order`: 4 distinct values.
All inputs are finite; a program needn't handle non-finite values.
Results may differ from a plain program's by a relative error of at most 0.013.
Values may be sent and summed in bfloat16 or wider, within the bound.
A program may use at most 64 MiB of HBM per device.

v0:
```python
import jax
import jax.numpy as jnp
from jax import lax
from jax.sharding import PartitionSpec as P

HEADS = 32
HD = 128


def partner(value, axis, distance):
    mask = 2**distance
    pairs = [(source, source ^ mask) for source in range(lax.axis_size(axis))]
    return lax.ppermute(value, axis, pairs)


def attend(carried, query_block, key_block, value_block, score_scale):
    running_max, running_sum, weighted = carried
    scores = (
        jnp.einsum("hqd,hkd->hqk", query_block, key_block, preferred_element_type=jnp.float32)
        * score_scale
    )
    new_max = jnp.maximum(running_max, jnp.max(scores, axis=-1))
    shrink = jnp.exp(running_max - new_max)
    weights = jnp.exp(scores - new_max[..., None])
    running_sum = running_sum * shrink + jnp.sum(weights, axis=-1)
    weighted = weighted * shrink[..., None] + jnp.einsum(
        "hqk,hkd->hqd",
        weights.astype(jnp.bfloat16),
        value_block,
        preferred_element_type=jnp.float32,
    )
    return (new_max, running_sum, weighted)


def masked_attend(carried, query_block, key_block, value_block, allowed, score_scale):
    return lax.cond(
        allowed,
        lambda held: attend(held, query_block, key_block, value_block, score_scale),
        lambda held: held,
        carried,
    )


def shards(query_vectors, key_vectors, value_vectors, levels, causal_order, level_gates):
    seq_count = lax.axis_size("seq")
    quarters = max(1, seq_count // HEADS)
    bit_count = quarters.bit_length() - 1
    tok_count = query_vectors.shape[1]
    part_len = tok_count // quarters
    score_scale = HD ** (-0.5)

    def to_heads(tensor):
        return (
            tensor.reshape(quarters, part_len, HEADS, HD)
            .transpose(2, 0, 1, 3)
            .reshape(HEADS * quarters, part_len, HD)
        )

    query_heads, key_heads, value_heads = (
        lax.all_to_all(to_heads(query_vectors), "seq", split_axis=0, concat_axis=1, tiled=True),
        lax.all_to_all(to_heads(key_vectors), "seq", split_axis=0, concat_axis=1, tiled=True),
        lax.all_to_all(to_heads(value_vectors), "seq", split_axis=0, concat_axis=1, tiled=True),
    )
    group_index = lax.axis_index("group")
    my_rank = lax.dynamic_index_in_dim(causal_order, group_index, keepdims=False)
    head_count = query_heads.shape[0]
    key_all, value_all = (
        lax.all_gather(key_heads[None], "group", axis=0, tiled=True),
        lax.all_gather(value_heads[None], "group", axis=0, tiled=True),
    )
    for bit_pos in range(bit_count):
        key_peer, value_peer = partner((key_all, value_all), "seq", bit_pos)
        key_all = jnp.concatenate([key_all, key_peer], axis=2)
        value_all = jnp.concatenate([value_all, value_peer], axis=2)
    row_count = query_heads.shape[1]
    carried = (
        jnp.full((head_count, row_count), -1e30, jnp.float32),
        jnp.zeros((head_count, row_count), jnp.float32),
        jnp.zeros((head_count, row_count, HD), jnp.float32),
    )
    for member in range(key_all.shape[0]):
        carried = masked_attend(
            carried,
            query_heads,
            key_all[member],
            value_all[member],
            causal_order[member] <= my_rank,
            score_scale,
        )
    running_max, running_sum, weighted = carried
    result = (weighted / running_sum[..., None]).astype(jnp.bfloat16)
    restored = lax.all_to_all(result, "seq", split_axis=1, concat_axis=0, tiled=True)
    restored = (
        restored.reshape(HEADS, quarters, part_len, HD)
        .transpose(1, 2, 0, 3)
        .reshape(tok_count, HEADS * HD)
    )
    level_index = lax.dynamic_index_in_dim(levels, group_index, keepdims=False)
    gate_row = lax.dynamic_index_in_dim(level_gates, level_index, keepdims=False)
    return (restored.astype(jnp.float32) * gate_row[None, :]).astype(jnp.bfloat16)[None]


def solution(mesh):
    placed = (
        P("group", "seq", None),
        P("group", "seq", None),
        P("group", "seq", None),
        P(),
        P(),
        P(),
    )
    return jax.shard_map(
        shards, mesh=mesh, in_specs=placed, out_specs=P("group", "seq", None), check_vma=False
    )
```

profile of v0, /device:TPU:5, one launch (start us, length us, event | category | flops | bytes accessed | tf_op | source)
XLA Modules:
  0.0 221.1 jit_solution(11040550291216581989)
XLA Ops:
  0.0 1.0 copy.34
  1.1 32.6 %all_to_all.19 = bf16[128,6,128]{2,1,0:T(8,128)(2,1)S(1)} all-to-all(bf16[128,6,128]{2,1,0:T(8,128)(2,1)S(1)} %bitcast.112), channel_id=1, replica_groups=mesh['group'=4,'seq'=128] {'seq'}, dimensions={0} | all-to-all | bytes 393216 | tf_op jit(solution)/shard_map/all_to_all | solution.py:62
  33.9 10.7 %all_gather.7 = bf16[4,1,768,128]{3,2,1,0:T(8,128)(2,1)S(1)} all-gather(bf16[1,1,768,128]{3,2,1,0:T(8,128)(2,1)S(1)} %broadcast_in_dim.38), channel_id=1, replica_groups=mesh['group'=4,'seq'=128] {'group'}, dimensions={0}, use_global_device_ids=true | all-gather | bytes 983040 | tf_op jit(solution)/shard_map/all_gather | solution.py:69
  44.6 3.9 %collective-permute-start.2 = (bf16[4,1,768,128]{3,2,1,0:T(8,128)(2,1)S(1)}, bf16[4,1,768,128]{3,2,1,0:T(8,128)(2,1)}, u32[]{:S(2)}, u32[]{:S(2)}) collective-permute-start(bf16[4,1,768,128]{3,2,1,0:T(8,128)(2,1)S(1)} %all_gather.7), channel_id=1, source_target_pairs={{0,1},{1,0},{2,3},{3,2},{4,5},{5,4},{6,7},{7,6},{8,9},{9,8},{10,11... | collective-permute-start | bytes 2359304 | tf_op jit(solution)/shard_map/ppermute | solution.py:13
  48.5 1.0 copy.33
  49.5 20.0 %all_to_all.40 = bf16[128,6,128]{2,1,0:T(8,128)(2,1)S(1)} all-to-all(bf16[128,6,128]{2,1,0:T(8,128)(2,1)S(1)} %bitcast.113), channel_id=1, replica_groups=mesh['group'=4,'seq'=128] {'seq'}, dimensions={0} | all-to-all | bytes 393216 | tf_op jit(solution)/shard_map/all_to_all | solution.py:61
  69.6 12.4 %all_gather.6 = bf16[4,1,768,128]{3,2,1,0:T(8,128)(2,1)S(1)} all-gather(bf16[1,1,768,128]{3,2,1,0:T(8,128)(2,1)S(1)} %broadcast_in_dim.32), channel_id=1, replica_groups=mesh['group'=4,'seq'=128] {'group'}, dimensions={0}, use_global_device_ids=true | all-gather | bytes 983040 | tf_op jit(solution)/shard_map/all_gather | solution.py:68
  82.1 3.9 %collective-permute-start = (bf16[4,1,768,128]{3,2,1,0:T(8,128)(2,1)S(1)}, bf16[4,1,768,128]{3,2,1,0:T(8,128)(2,1)}, u32[]{:S(2)}, u32[]{:S(2)}) collective-permute-start(bf16[4,1,768,128]{3,2,1,0:T(8,128)(2,1)S(1)} %all_gather.6), channel_id=1, source_target_pairs={{0,1},{1,0},{2,3},{3,2},{4,5},{5,4},{6,7},{7,6},{8,9},{9,8},{10,11... | collective-permute-start | bytes 2359304 | tf_op jit(solution)/shard_map/ppermute | solution.py:13
  86.0 2.4 %pad_maximum_fusion.1 = bf16[4,1,1536,128]{3,2,1,0:T(8,128)(2,1)} fusion(bf16[4,1,768,128]{3,2,1,0:T(8,128)(2,1)} %collective-permute-done.2, bf16[4,1,768,128]{3,2,1,0:T(8,128)(2,1)S(1)} %all_gather.7), kind=kLoop, calls=%fused_computation.69 | loop fusion | flops 3145728 | bytes 3145728 | tf_op jit(solution)/shard_map/concatenate | solution.py:74
  88.4 2.4 %collective-permute-start.3 = (bf16[4,1,1536,128]{3,2,1,0:T(8,128)(2,1)}, bf16[4,1,1536,128]{3,2,1,0:T(8,128)(2,1)}, u32[]{:S(2)}, u32[]{:S(2)}) collective-permute-start(bf16[4,1,1536,128]{3,2,1,0:T(8,128)(2,1)} %pad_maximum_fusion.1), channel_id=1, source_target_pairs={{0,2},{1,3},{2,0},{3,1},{4,6},{5,7},{6,4},{7,5},{8,10},{9,11},{10,... | collective-permute-start | bytes 4718600 | tf_op jit(solution)/shard_map/ppermute | solution.py:13
  90.8 1.0 copy.32
  91.7 0.8 copy.24
  92.5 5.4 %all-to-all-start = ((bf16[128,6,128]{2,1,0:T(8,128)(2,1)}), bf16[128,6,128]{2,1,0:T(8,128)(2,1)S(1)}, u32[]{:S(2)}, u32[]{:S(2)}) async-start(bf16[128,6,128]{2,1,0:T(8,128)(2,1)} %bitcast.21), calls=%async_computation | async-start | bytes 524288 | tf_op jit(solution)/shard_map/all_to_all | solution.py:60
  98.0 2.4 %pad_maximum_fusion = bf16[4,1,1536,128]{3,2,1,0:T(8,128)(2,1)} fusion(bf16[4,1,768,128]{3,2,1,0:T(8,128)(2,1)} %collective-permute-done, bf16[4,1,768,128]{3,2,1,0:T(8,128)(2,1)S(1)} %all_gather.6), kind=kLoop, calls=%fused_computation.68 | loop fusion | flops 3145728 | bytes 3145728 | tf_op jit(solution)/shard_map/concatenate | solution.py:73
  100.4 3.3 %collective-permute-start.1 = (bf16[4,1,1536,128]{3,2,1,0:T(8,128)(2,1)}, bf16[4,1,1536,128]{3,2,1,0:T(8,128)(2,1)}, u32[]{:S(2)}, u32[]{:S(2)}) collective-permute-start(bf16[4,1,1536,128]{3,2,1,0:T(8,128)(2,1)} %pad_maximum_fusion), channel_id=1, source_target_pairs={{0,2},{1,3},{2,0},{3,1},{4,6},{5,7},{6,4},{7,5},{8,10},{9,11},{10,... | collective-permute-start | bytes 4718600 | tf_op jit(solution)/shard_map/ppermute | solution.py:13
  103.7 0.7 fusion.68
  109.1 0.6 dynamic_slice.12
  111.4 22.1 %all-to-all-done = bf16[128,6,128]{2,1,0:T(8,128)(2,1)S(1)} async-done(((bf16[128,6,128]{2,1,0:T(8,128)(2,1)}), bf16[128,6,128]{2,1,0:T(8,128)(2,1)S(1)}, u32[]{:S(2)}, u32[]{:S(2)}) %all-to-all-start) | async-done | bytes 196640 | tf_op jit(solution)/shard_map/all_to_all | solution.py:60
  133.6 1.2 constant_dynamic-update-slice_fusion.4
  134.9 1.2 constant_dynamic-update-slice_fusion.1
  136.1 1.6 constant_dynamic-update-slice_fusion.3
  137.9 28.0 %collective-permute-done.1 = bf16[4,1,1536,128]{3,2,1,0:T(8,128)(2,1)} collective-permute-done((bf16[4,1,1536,128]{3,2,1,0:T(8,128)(2,1)}, bf16[4,1,1536,128]{3,2,1,0:T(8,128)(2,1)}, u32[]{:S(2)}, u32[]{:S(2)}) %collective-permute-start.1) | collective-permute-done | bytes 1572896 | tf_op jit(solution)/shard_map/ppermute | solution.py:13
  165.9 1.6 constant_dynamic-update-slice_fusion
  167.6 1.6 copy-done.2
  169.2 5.4 %conditional.4 = (f32[1,768]{1,0:T(1,128)S(1)}, f32[1,768]{1,0:T(1,128)S(1)}, f32[1,768,128]{2,1,0:T(8,128)S(1)}) conditional(s32[]{:T(128)} %bitcast.19, () %tuple.32, (bf16[1,768,128]{2,1,0:T(8,128)(2,1)S(1)}, bf16[1,3072,128]{2,1,0:T(8,128)(2,1)S(1)}, bf16[1,3072,128]{2,1,0:T(8,128)(2,1)S(1)}) %tuple.33), branch_computations={%region_0.1_spmd, %region_1.4_spmd} | conditional | flops 1226935296 | bytes 30514200 | solution.py:36
  169.2 1.5 multiply_reduce_fusion
  170.7 1.7 fusion.1
  172.4 2.2 %fusion.7 = f32[1,768,128]{2,1,0:T(8,128)S(1)} fusion(f32[768,3072]{1,0:T(8,128)S(1)} %get-tuple-element.125, f32[768]{0:T(1024)S(1)} %get-tuple-element.123, bf16[1,3072,128]{2,1,0:T(8,128)(2,1)S(1)} %get-tuple-element.73, f32[768]{0:T(1024)S(1)} %get-tuple-element.122), kind=kOutput, calls=%fused_computation.6 | convolution fusion | flops 611155968 | bytes 10622976 | tf_op jit(solution)/shard_map/cond/branch_1_fun/hqk,hkd->hqd/dot_general | solution.py:26
  174.6 5.4 %conditional.5 = ((f32[1,768]{1,0:T(1,128)S(1)}, f32[1,768]{1,0:T(1,128)S(1)}, f32[1,768,128]{2,1,0:T(8,128)S(1)})) conditional(s32[]{:T(128)} %bitcast.18, (f32[1,768]{1,0:T(1,128)S(1)}, f32[1,768]{1,0:T(1,128)S(1)}, f32[1,768,128]{2,1,0:T(8,128)S(1)}) %conditional.4, (bf16[1,768,128]{2,1,0:T(8,128)(2,1)S(1)}, bf16[1,3072,128]{2,1,0:T(8,128)(2,1)S(1)}, ...), branch_computations={%region_4.5_spmd, %region_5.8_spmd} | conditional | flops 1227032832 | bytes 30919712 | solution.py:36
  174.7 1.5 multiply_reduce_fusion.1
  176.2 1.7 fusion.16
  177.8 2.2 %fusion.22 = f32[1,768,128]{2,1,0:T(8,128)S(1)} fusion(f32[768,3072]{1,0:T(8,128)S(1)} %get-tuple-element.129, f32[768]{0:T(1024)S(1)} %get-tuple-element.115, bf16[1,3072,128]{2,1,0:T(8,128)(2,1)S(1)} %get-tuple-element.79, f32[1,768,128]{2,1,0:T(8,128)S(1)} %get-tuple-element.78, f32[768]{0:T(1024)S(1)} %get-tuple-element.114), kind=kOutput, calls=%fused_computation.21 | convolution fusion | flops 611254272 | bytes 11016192 | tf_op jit(solution)/shard_map/cond/branch_1_fun/hqk,hkd->hqd/dot_general | solution.py:26
  180.1 7.5 %conditional.6 = ((f32[1,768]{1,0:T(1,128)S(1)}, f32[1,768]{1,0:T(1,128)S(1)}, f32[1,768,128]{2,1,0:T(8,128)S(1)})) conditional(s32[]{:T(128)} %bitcast.17, (f32[1,768]{1,0:T(1,128)S(1)}, f32[1,768]{1,0:T(1,128)S(1)}, f32[1,768,128]{2,1,0:T(8,128)S(1)}) %get-tuple-element.163, (bf16[1,768,128]{2,1,0:T(8,128)(2,1)S(1)}, ...), branch_computations={%region_8.9_spmd, %region_9.12_spmd} | conditional | flops 1227032832 | bytes 30919712 | solution.py:36
  180.3 2.6 %multiply_reduce_fusion.2 = (f32[768]{0:T(1024)S(1)}, f32[768,3072]{1,0:T(8,128)S(1)}) fusion(bf16[4,1,3072,128]{3,2,1,0:T(8,128)(2,1)} %get-tuple-element.82, bf16[1,768,128]{2,1,0:T(8,128)(2,1)S(1)} %get-tuple-element.81), kind=kOutput, calls=%fused_computation.32 | convolution fusion | flops 608697600 | bytes 10423296 | tf_op jit(solution)/shard_map/cond/branch_1_fun/hqd,hkd->hqk/dot_general | solution.py:19
  182.9 1.7 fusion.32
  184.6 2.9 %fusion.38 = f32[1,768,128]{2,1,0:T(8,128)S(1)} fusion(f32[768,3072]{1,0:T(8,128)S(1)} %get-tuple-element.131, f32[768]{0:T(1024)S(1)} %get-tuple-element.117, bf16[4,1,3072,128]{3,2,1,0:T(8,128)(2,1)} %get-tuple-element.85, f32[1,768,128]{2,1,0:T(8,128)S(1)} %get-tuple-element.84, f32[768]{0:T(1024)S(1)} %get-tuple-element.116), kind=kOutput, calls=%fused_computation.37 | convolution fusion | flops 611254272 | bytes 11016192 | tf_op jit(solution)/shard_map/cond/branch_1_fun/hqk,hkd->hqd/dot_general | solution.py:26
  187.5 7.2 %conditional.7 = ((f32[1,768]{1,0:T(1,128)S(1)}, f32[1,768,128]{2,1,0:T(8,128)S(1)})) conditional(s32[]{:T(128)} %bitcast.16, (f32[1,768]{1,0:T(1,128)S(1)}, f32[1,768,128]{2,1,0:T(8,128)S(1)}) %tuple.36, (bf16[1,768,128]{2,1,0:T(8,128)(2,1)S(1)}, bf16[4,1,3072,128]{3,2,1,0:T(8,128)(2,1)}, f32[1,768]{1,0:T(1,128)S(1)}, f32[1,768]{1,0:T(1,128)S(1)}, ...), branch_computations={%region_12.13_spmd, %region_13.16_spmd} | conditional | flops 1227033600 | bytes 30910488 | solution.py:36
  187.6 2.6 %multiply_reduce_fusion.3 = (f32[768]{0:T(1024)S(1)}, f32[768,3072]{1,0:T(8,128)S(1)}) fusion(bf16[4,1,3072,128]{3,2,1,0:T(8,128)(2,1)} %get-tuple-element.89, bf16[1,768,128]{2,1,0:T(8,128)(2,1)S(1)} %get-tuple-element.88), kind=kOutput, calls=%fused_computation.50 | convolution fusion | flops 608697600 | bytes 10423296 | tf_op jit(solution)/shard_map/cond/branch_1_fun/hqd,hkd->hqk/dot_general | solution.py:19
  190.2 2.9 %fusion.56 = f32[1,768,128]{2,1,0:T(8,128)S(1)} fusion(f32[768,3072]{1,0:T(8,128)S(1)} %get-tuple-element.127, f32[768]{0:T(1024)S(1)} %get-tuple-element.119, bf16[4,1,3072,128]{3,2,1,0:T(8,128)(2,1)} %get-tuple-element.91, f32[1,768,128]{2,1,0:T(8,128)S(1)} %get-tuple-element.90, f32[768]{0:T(1024)S(1)} %get-tuple-element.118), kind=kOutput, calls=%fused_computation.55 | convolution fusion | flops 611254272 | bytes 11016192 | tf_op jit(solution)/shard_map/cond/branch_1_fun/hqk,hkd->hqd/dot_general | solution.py:26
  193.1 1.7 fusion.50
  195.0 0.3 copy.36
  195.3 0.5 broadcast.138
  195.8 1.8 reduce.33
  197.6 0.8 reshape.268
  198.4 6.2 %all-to-all-start.3 = ((bf16[128,2,384]{2,1,0:T(2,128)(2,1)}), bf16[128,2,384]{2,1,0:T(2,128)(2,1)S(1)}, u32[]{:S(2)}, u32[]{:S(2)}) async-start(bf16[128,2,384]{2,1,0:T(2,128)(2,1)} %reshape.268), calls=%async_computation.3 | async-start | bytes 393216 | tf_op jit(solution)/shard_map/all_to_all | solution.py:92
  204.7 14.1 %all-to-all-done.3 = bf16[128,2,384]{2,1,0:T(2,128)(2,1)S(1)} async-done(((bf16[128,2,384]{2,1,0:T(2,128)(2,1)}), bf16[128,2,384]{2,1,0:T(2,128)(2,1)S(1)}, u32[]{:S(2)}, u32[]{:S(2)}) %all-to-all-start.3) | async-done | bytes 196640 | tf_op jit(solution)/shard_map/all_to_all | solution.py:92
  218.9 1.1 convert_reduce_fusion
  220.4 0.7 multiply_convert_fusion
  (39 shorter events, 1.6 us)
Async XLA Ops:
  0.0 204.6 %copy-start = (f32[50,4096]{1,0:T(8,128)S(1)}, f32[50,4096]{1,0:T(8,128)}, u32[]{:S(2)}) copy-start(f32[50,4096]{1,0:T(8,128)} %param.19) | copy-start | bytes 2457604
  0.0 103.7 %copy-start.3 = (s32[4]{0:T(128)S(1)}, s32[4]{0:T(128)}, u32[]{:S(2)}) copy-start(s32[4]{0:T(128)} %param.18) | copy-start | bytes 52
  0.0 109.1 %copy-start.4 = (s32[4]{0:T(128)S(1)}, s32[4]{0:T(128)}, u32[]{:S(2)}) copy-start(s32[4]{0:T(128)} %param.17) | copy-start | bytes 52
  44.6 41.4 %collective-permute-start.2 = (bf16[4,1,768,128]{3,2,1,0:T(8,128)(2,1)S(1)}, bf16[4,1,768,128]{3,2,1,0:T(8,128)(2,1)}, u32[]{:S(2)}, u32[]{:S(2)}) collective-permute-start(bf16[4,1,768,128]{3,2,1,0:T(8,128)(2,1)S(1)} %all_gather.7), channel_id=1, source_target_pairs={{0,1},{1,0},{2,3},{3,2},{4,5},{5,4},{6,7},{7,6},{8,9},{9,8},{10,11... | collective-permute-start | bytes 2359304 | tf_op jit(solution)/shard_map/ppermute | solution.py:13
  82.1 15.9 %collective-permute-start = (bf16[4,1,768,128]{3,2,1,0:T(8,128)(2,1)S(1)}, bf16[4,1,768,128]{3,2,1,0:T(8,128)(2,1)}, u32[]{:S(2)}, u32[]{:S(2)}) collective-permute-start(bf16[4,1,768,128]{3,2,1,0:T(8,128)(2,1)S(1)} %all_gather.6), channel_id=1, source_target_pairs={{0,1},{1,0},{2,3},{3,2},{4,5},{5,4},{6,7},{7,6},{8,9},{9,8},{10,11... | collective-permute-start | bytes 2359304 | tf_op jit(solution)/shard_map/ppermute | solution.py:13
  88.4 47.8 %collective-permute-start.3 = (bf16[4,1,1536,128]{3,2,1,0:T(8,128)(2,1)}, bf16[4,1,1536,128]{3,2,1,0:T(8,128)(2,1)}, u32[]{:S(2)}, u32[]{:S(2)}) collective-permute-start(bf16[4,1,1536,128]{3,2,1,0:T(8,128)(2,1)} %pad_maximum_fusion.1), channel_id=1, source_target_pairs={{0,2},{1,3},{2,0},{3,1},{4,6},{5,7},{6,4},{7,5},{8,10},{9,11},{10,... | collective-permute-start | bytes 4718600 | tf_op jit(solution)/shard_map/ppermute | solution.py:13
  92.5 40.9 %all-to-all-start = ((bf16[128,6,128]{2,1,0:T(8,128)(2,1)}), bf16[128,6,128]{2,1,0:T(8,128)(2,1)S(1)}, u32[]{:S(2)}, u32[]{:S(2)}) async-start(bf16[128,6,128]{2,1,0:T(8,128)(2,1)} %bitcast.21), calls=%async_computation | async-start | bytes 524288 | tf_op jit(solution)/shard_map/all_to_all | solution.py:60
  100.4 65.5 %collective-permute-start.1 = (bf16[4,1,1536,128]{3,2,1,0:T(8,128)(2,1)}, bf16[4,1,1536,128]{3,2,1,0:T(8,128)(2,1)}, u32[]{:S(2)}, u32[]{:S(2)}) collective-permute-start(bf16[4,1,1536,128]{3,2,1,0:T(8,128)(2,1)} %pad_maximum_fusion), channel_id=1, source_target_pairs={{0,2},{1,3},{2,0},{3,1},{4,6},{5,7},{6,4},{7,5},{8,10},{9,11},{10,... | collective-permute-start | bytes 4718600 | tf_op jit(solution)/shard_map/ppermute | solution.py:13
  137.7 29.9 %copy-start.1 = (bf16[4,1,3072,128]{3,2,1,0:T(8,128)(2,1)}, bf16[4,1,3072,128]{3,2,1,0:T(8,128)(2,1)S(1)}, u32[]{:S(2)}) copy-start(bf16[4,1,3072,128]{3,2,1,0:T(8,128)(2,1)S(1)} %constant_dynamic-update-slice_fusion.3) | copy-start | bytes 9437188
  167.5 1.7 copy-start.2
  198.4 20.3 %all-to-all-start.3 = ((bf16[128,2,384]{2,1,0:T(2,128)(2,1)}), bf16[128,2,384]{2,1,0:T(2,128)(2,1)S(1)}, u32[]{:S(2)}, u32[]{:S(2)}) async-start(bf16[128,2,384]{2,1,0:T(2,128)(2,1)} %reshape.268), calls=%async_computation.3 | async-start | bytes 393216 | tf_op jit(solution)/shard_map/all_to_all | solution.py:92
where the time goes:
time: 222 us; the launch traced here: 221 us
  blocking collectives  75.8 us (34%)
  waiting for transfers between devices  64.2 us (29%)
  starting transfers between devices  25.1 us (11%)
  matrix products  18.4 us (8%)
  other arithmetic  15.4 us (7%)
  local copies, waits for them, and re-layouts  15.1 us (7%)
  between operations  6.76 us (3%)
    all_to_all x1, blocking collectives, shards(): lax.all_to_all(to_heads(value_vectors), 'seq', split_axis=0, concat_axis=...  32.6 us
    ppermute x4, waiting for transfers between devices, partner(): return lax.ppermute(value, axis, pairs)  28 us
    all_to_all x1, waiting for transfers between devices, shards(): lax.all_to_all(to_heads(query_vectors), 'seq', split_axis=0, concat_axis=...  22.1 us
    all_to_all x1, blocking collectives, shards(): lax.all_to_all(to_heads(key_vectors), 'seq', split_axis=0, concat_axis=1,...  20 us
    all_to_all x1, waiting for transfers between devices, shards(): lax.all_to_all(result, 'seq', split_axis=1, concat_axis=0, tiled=True)  14.1 us
    ppermute x4, starting transfers between devices, partner(): return lax.ppermute(value, axis, pairs)  13.5 us
    all_gather x1, blocking collectives, shards(): lax.all_gather(key_heads[None], 'group', axis=0, tiled=True)  12.4 us
    all_gather x1, blocking collectives, shards(): lax.all_gather(value_heads[None], 'group', axis=0, tiled=True)  10.7 us
  transfers between devices with their start and end apart: 6, of which 3 were waited for; matrix products, arithmetic and copies ran while one was open for 6% of the time, Pallas kernels for 0%

commit v1 on v0

v1 whole, which is shorter than its diff:
```python
import jax
import jax.numpy as jnp
from jax import lax
from jax.experimental import pallas as pl
from jax.experimental.pallas import tpu as pltpu
from jax.sharding import PartitionSpec as P

HEADS = 32
HD = 128
GROUPS = 4
ROWS = 24
PAD = 32
SLOTS = 32
PART = 192
SUBSETS = 4
FOLD = HD**-0.5 * 1.4426950408889634
BF16, F32 = jnp.bfloat16, jnp.float32
MESH = pl.DeviceIdType.MESH
VMEM = pl.BlockSpec(memory_space=pltpu.VMEM)
SMEM = pl.BlockSpec(memory_space=pltpu.SMEM)


class Place:
    def __init__(self):
        seq = lax.axis_index("seq")
        self.x = lax.axis_index("group")
        self.core = seq % 2
        self.y = (seq // 2) % 8
        self.z = seq // 16
        self.pair, self.j = self.y // 2, self.y % 2

    def at(self, x, y, z, core):
        return {"group": x % 4, "seq": ((z % 8) * 8 + y % 8) * 2 + core}

    def target(self, dz, r):
        pair = (self.pair + r) % 4
        e = (self.y - 2 * pair + 7) % 8
        j = 1 - e // 4
        slot = j * e + (1 - j) * (7 - e)
        z = (self.z - dz) % 8
        return z * 4 + pair, 2 * pair + j, z, dz * 4 + slot

    def source(self, dz, slot):
        return (self.y + (2 * self.j - 1) * slot + 8) % 8, (self.z + dz) % 8


def remote(src, dst, send, recv, device):
    return pltpu.make_async_remote_copy(src, dst, send, recv, device_id=device, device_id_type=MESH)


def landed(ref, sem):
    pltpu.make_async_copy(ref, ref, sem).wait()


def head_columns(head):
    return pl.ds(pl.multiple_of(head * HD, HD), HD)


def side_by_side(two):
    return jnp.concatenate([two[0].astype(F32), two[1].astype(F32)], axis=0).astype(BF16)


def gather_kernel(
    q_ref, k_ref, v_ref, q_all, kv_all, q_stage, kv_stage, q_got, kv_got, send_sem, q_sem, kv_sem, near_sem, far_sem, core_sem, pair_sem
):
    me = Place()
    x, y, z, core = me.x, me.y, me.z, me.core
    right, left = me.at(x + 1, y, z, core), me.at(x + 3, y, z, core)
    other_core = me.at(x, y, z, 1 - core)
    partner = me.at(x, y + 1 - 2 * me.j, z, core)

    barrier = pltpu.get_barrier_semaphore()

    def greet(device):
        pl.semaphore_signal(barrier, inc=1, device_id=device, device_id_type=MESH)

    def greet_kv(i, carry):
        ys, zs = me.source(i // 4, i % 4)
        greet(me.at(x, ys, zs, core))
        return carry

    def greet_q(i, carry):
        dz = i // 4
        ys, zs = me.source(dz, i % 4)
        greet(me.at(x - dz + 8, ys, zs, core))
        return carry

    lax.fori_loop(1, SLOTS, greet_kv, 0)
    lax.fori_loop(4, 16, greet_q, 0)
    lax.fori_loop(20, SLOTS, greet_q, 0)
    for device in (right, left, other_core, partner):
        greet(device)

    def stage(h, carry):
        columns = head_columns(h)
        q_stage[h, :ROWS] = q_ref[0, :, columns]
        q_stage[h, ROWS:] = jnp.zeros((PAD - ROWS, HD), BF16)
        kv_stage[h] = side_by_side((k_ref[0, :, columns], v_ref[0, :, columns]))
        return carry

    lax.fori_loop(0, HEADS, stage, 0)
    own = z * 4 + me.pair
    q_got[0] = q_stage[own]
    kv_got[0] = kv_stage[own]
    pl.semaphore_wait(barrier, 31 + 24 + 4)

    def send_q(i, carry):
        dz = i // 4
        head, yd, zd, slot = me.target(dz, i % 4)
        remote(q_stage.at[head], q_got.at[slot], send_sem.at[0], q_sem, me.at(x + dz, yd, zd, core)).start()
        return carry

    def send_kv(i, carry):
        dz = i // 4
        head, yd, zd, slot = me.target(dz, i % 4)
        remote(kv_stage.at[head], kv_got.at[slot], send_sem.at[1], kv_sem.at[dz // 2], me.at(x, yd, zd, core)).start()
        return carry

    lax.fori_loop(1, SLOTS, send_kv, 0)
    lax.fori_loop(1, SLOTS, send_q, 0)

    def block(group, t, which):
        return kv_all.at[group, :, t, which]

    sent = []

    def push(src, dst, sem, recv, device):
        copy = remote(src, dst, sem, recv, device)
        copy.start()
        sent.append(copy)

    def own_part(t):
        first = 1 if t == 0 else 0
        landed(kv_got.at[pl.ds(t * 8 + first, 8 - first)], kv_sem.at[t])
        for i in range(4):
            two = kv_got[t * 8 + 2 * i], kv_got[t * 8 + 2 * i + 1]
            rows = pl.ds(i * 48, 48)
            kv_all[x, 0, t, core, rows] = side_by_side((two[0][:ROWS], two[1][:ROWS]))
            kv_all[x, 1, t, core, rows] = side_by_side((two[0][ROWS:], two[1][ROWS:]))
        mine = block(x, t, core)
        push(mine, mine, send_sem.at[2 + t], near_sem.at[0, t], right)
        push(mine, mine, send_sem.at[6 + t], near_sem.at[1, t], left)
        push(mine, mine, send_sem.at[10 + t], core_sem.at[0, t], other_core)

    def forward(t):
        from_left, from_right = (x + 3) % 4, (x + 1) % 4
        landed(block(from_left, t, core), near_sem.at[0, t])
        keys = kv_all.at[from_left, 0, t, core]
        push(keys, keys, send_sem.at[14 + t], far_sem.at[0, t], right)
        held = block(from_left, t, core)
        push(held, held, send_sem.at[18 + t], core_sem.at[1, t], other_core)
        landed(block(from_right, t, core), near_sem.at[1, t])
        values = kv_all.at[from_right, 1, t, core]
        push(values, values, send_sem.at[22 + t], far_sem.at[1, t], left)
        held = block(from_right, t, core)
        push(held, held, send_sem.at[26 + t], core_sem.at[2, t], other_core)

    def last(t):
        far = (x + 2) % 4
        landed(kv_all.at[far, 0, t, core], far_sem.at[0, t])
        landed(kv_all.at[far, 1, t, core], far_sem.at[1, t])
        held = block(far, t, core)
        push(held, held, send_sem.at[30 + t], core_sem.at[3, t], other_core)

    for step in range(SUBSETS + 2):
        if step < SUBSETS:
            own_part(step)
        if 0 <= step - 1 < SUBSETS:
            forward(step - 1)
        if 0 <= step - 2 < SUBSETS:
            last(step - 2)

    landed(q_got.at[pl.ds(1, SLOTS - 1)], q_sem)
    for dz in range(4):
        group = (x + 4 - dz) % 4
        for i in range(4):
            slot = dz * 4 + (i // 2) * 16 + (i % 2) * 2
            two = q_got[slot, :ROWS], q_got[slot + 1, :ROWS]
            q_all[me.j, group, pl.ds(i * 48, 48)] = side_by_side(two)
    push(q_all.at[me.j], q_all.at[me.j], send_sem.at[34], pair_sem, partner)

    for t in range(SUBSETS):
        for i, dx in enumerate((0, 3, 1, 2)):
            landed(block((x + dx) % 4, t, 1 - core), core_sem.at[i, t])
    landed(q_all.at[1 - me.j], pair_sem)
    landed(q_stage.at[pl.ds(1, SLOTS - 1)], send_sem.at[0])
    landed(kv_stage.at[pl.ds(1, SLOTS - 1)], send_sem.at[1])
    for copy in sent:
        copy.wait_send()


def gather(q, k, v):
    return pl.pallas_call(
        gather_kernel,
        out_shape=(
            jax.ShapeDtypeStruct((2, GROUPS, PART, HD), BF16),
            jax.ShapeDtypeStruct((GROUPS, 2, SUBSETS, 2, PART, HD), BF16),
        ),
        in_specs=[VMEM] * 3,
        out_specs=(VMEM, VMEM),
        scratch_shapes=[
            pltpu.VMEM((HEADS, PAD, HD), BF16),
            pltpu.VMEM((HEADS, 2 * ROWS, HD), BF16),
            pltpu.VMEM((SLOTS, PAD, HD), BF16),
            pltpu.VMEM((SLOTS, 2 * ROWS, HD), BF16),
            pltpu.SemaphoreType.DMA((35,)),
            pltpu.SemaphoreType.DMA,
            pltpu.SemaphoreType.DMA((SUBSETS,)),
            pltpu.SemaphoreType.DMA((2, SUBSETS)),
            pltpu.SemaphoreType.DMA((2, SUBSETS)),
            pltpu.SemaphoreType.DMA((4, SUBSETS)),
            pltpu.SemaphoreType.DMA,
        ],
        compiler_params=pltpu.CompilerParams(collective_id=0, has_side_effects=True, vmem_limit_bytes=48 * 2**20),
        name="gather",
    )(q, k, v)


def attend_kernel(order_ref, q_ref, kv_ref, o_ref, lse_ref, kk_ref, vv_ref):
    ranks = []
    for g in range(GROUPS):
        ranks.append(sum((order_ref[o] < order_ref[g]).astype(jnp.int32) for o in range(GROUPS)))
    at_rank = [sum(jnp.where(ranks[g] == r, g, 0) for g in range(GROUPS)) for r in range(GROUPS)]
    keys = kv_ref.shape[2]
    for r in range(GROUPS):
        k = kv_ref[at_rank[r], 0]
        kk_ref[r] = jnp.concatenate([k, k], axis=1)
        vv_ref[r] = jnp.concatenate([kv_ref[at_rank[r], 1], jnp.ones((keys, HD), BF16)], axis=1)
    for r in range(GROUPS):
        group = at_rank[r]
        for j in range(2):
            q = q_ref[j, group].astype(F32) * FOLD
            high = q.astype(BF16)
            q = jnp.concatenate([high, (q - high.astype(F32)).astype(BF16)], axis=1)
            top = total = None
            for other in range(r + 1):
                scores = lax.dot_general(q, kk_ref[other], (((1,), (1,)), ((), ())), preferred_element_type=F32)
                new_top = jnp.max(scores, axis=-1, keepdims=True)
                if other:
                    new_top = jnp.maximum(top, new_top)
                weights = jnp.exp2(scores - new_top).astype(BF16)
                mixed = jnp.dot(weights, vv_ref[other], preferred_element_type=F32)
                total = mixed if other == 0 else total * jnp.exp2(top - new_top) + mixed
                top = new_top
            row_sum = total[:, HD : HD + 1]
            o_ref[j, group] = total[:, :HD] / row_sum
            lse = top + jnp.log2(row_sum)
            for i in range(0, PART, 64):
                lse_ref[j, group, pl.ds(i // 64, 1)] = to_lanes(lse[i : i + 64])


def diagonal():
    return lax.broadcasted_iota(jnp.int32, (64, HD), 0) == lax.broadcasted_iota(jnp.int32, (64, HD), 1)


def to_lanes(column):
    return jnp.sum(jnp.where(diagonal(), column, 0.0), axis=0, keepdims=True)


def to_column(lanes):
    return jnp.sum(jnp.where(diagonal(), lanes, 0.0), axis=1, keepdims=True)


def attend(order, q, kv):
    kv = kv.reshape(GROUPS, 2, SUBSETS * 2 * PART, HD)
    keys = kv.shape[2]
    return pl.pallas_call(
        attend_kernel,
        out_shape=(
            jax.ShapeDtypeStruct((2, GROUPS, PART, HD), F32),
            jax.ShapeDtypeStruct((2, GROUPS, 8, HD), F32),
        ),
        in_specs=[SMEM, VMEM, VMEM],
        out_specs=(VMEM, VMEM),
        scratch_shapes=[
            pltpu.VMEM((GROUPS, keys, 2 * HD), BF16),
            pltpu.VMEM((GROUPS, keys, 2 * HD), BF16),
        ],
        compiler_params=pltpu.CompilerParams(vmem_limit_bytes=48 * 2**20),
        name="attend",
    )(order, q, kv)


def scatter_kernel(o_ref, lse_ref, out_ref, o_out, o_in, lse_out, lse_in, stage_ref, got, sems, home_sem):
    me = Place()
    x, y, z, core = me.x, me.y, me.z, me.core
    partner = me.at(x, y + 1 - 2 * me.j, z, core)
    barrier = pltpu.get_barrier_semaphore()

    def greet(i, carry):
        dz = i // 4
        _, yd, zd, _ = me.target(dz, i % 4)
        pl.semaphore_signal(barrier, inc=1, device_id=me.at(x + dz, yd, zd, core), device_id_type=MESH)
        return carry

    lax.fori_loop(1, SLOTS, greet, 0)
    pl.semaphore_signal(barrier, inc=1, device_id=partner, device_id_type=MESH)
    for g in range(GROUPS):
        o_out[g] = o_ref[1 - me.j, g].astype(BF16)
        lse_out[g] = lse_ref[1 - me.j, g]
    pl.semaphore_wait(barrier, SLOTS)
    give_o = remote(o_out, o_in, sems.at[0], sems.at[1], partner)
    give_lse = remote(lse_out, lse_in, sems.at[2], sems.at[3], partner)
    give_lse.start()
    give_o.start()
    give_lse.wait()
    give_o.wait()
    for dz in range(4):
        group = (x + 4 - dz) % 4
        for i in range(3):
            rows = pl.ds(i * 64, 64)
            difference = lse_in[group, pl.ds(i, 1)] - lse_ref[me.j, group, pl.ds(i, 1)]
            weight = to_column(1.0 / (1.0 + jnp.exp2(difference)))
            theirs = o_in[group, rows].astype(F32)
            o_ref_rows = o_ref[me.j, group, rows]
            merged = theirs + (o_ref_rows - theirs) * weight
            for part in range(8):
                run = i * 8 + part
                slot = dz * 4 + (run // 12) * 16 + (run // 3) % 4
                stage_ref[slot, pl.ds((run % 3) * 8, 8)] = merged[part * 8 : part * 8 + 8].astype(BF16)
        for i in range(8):
            stage_ref[dz * 4 + (i // 4) * 16 + i % 4, ROWS:] = jnp.zeros((PAD - ROWS, HD), BF16)
    own = z * 4 + me.pair
    got[own] = stage_ref[0]

    def send(i, carry):
        dz = i // 4
        ys, zs = me.source(dz, i % 4)
        remote(stage_ref.at[i], got.at[own], sems.at[4], home_sem, me.at(x - dz + 8, ys, zs, core)).start()
        return carry

    lax.fori_loop(1, SLOTS, send, 0)
    landed(got.at[pl.ds(1, SLOTS - 1)], home_sem)
    for h in range(HEADS):
        out_ref[:, h * HD : (h + 1) * HD] = got[h, :ROWS]
    landed(stage_ref.at[pl.ds(1, SLOTS - 1)], sems.at[4])


def scatter(o, lse):
    return pl.pallas_call(
        scatter_kernel,
        out_shape=jax.ShapeDtypeStruct((ROWS, HEADS * HD), BF16),
        in_specs=[VMEM, VMEM],
        out_specs=VMEM,
        scratch_shapes=[
            pltpu.VMEM((GROUPS, PART, HD), BF16),
            pltpu.VMEM((GROUPS, PART, HD), BF16),
            pltpu.VMEM((GROUPS, 8, HD), F32),
            pltpu.VMEM((GROUPS, 8, HD), F32),
            pltpu.VMEM((SLOTS, PAD, HD), BF16),
            pltpu.VMEM((HEADS, PAD, HD), BF16),
            pltpu.SemaphoreType.DMA((5,)),
            pltpu.SemaphoreType.DMA,
        ],
        compiler_params=pltpu.CompilerParams(collective_id=1, has_side_effects=True, vmem_limit_bytes=48 * 2**20),
        name="scatter",
    )(o, lse)


def shards(query_vectors, key_vectors, value_vectors, levels, causal_order, level_gates):
    q, kv = gather(query_vectors, key_vectors, value_vectors)
    joined = scatter(*attend(causal_order, q, kv))
    level = lax.dynamic_index_in_dim(levels, lax.axis_index("group"), keepdims=False)
    gate_row = lax.dynamic_index_in_dim(level_gates, level, keepdims=False)
    return (joined.astype(F32) * gate_row[None, :]).astype(BF16)[None]


def solution(mesh):
    placed = P("group", "seq", None)
    return jax.shard_map(
        shards, mesh=mesh, in_specs=(placed, placed, placed, P(), P(), P()), out_specs=placed, check_vma=False
    )
```

time: 222 us -> 95.4 us (0.43)
  the two profiles are of different devices: /device:TPU:5 before, /device:TPU:8 now
where the time goes in v1:
time: 95.4 us; the launch traced here: 95.1 us
  Pallas kernels  88.3 us (93%)
  local copies, waits for them, and re-layouts  4.13 us (4%)
  between operations  2.01 us (2%)
    pallas_call x1, Pallas kernels, gather(): pl.pallas_call(gather_kernel, out_shape=(jax.ShapeDtypeStruct((2, GROUPS,...  50.9 us
    pallas_call x1, Pallas kernels, scatter(): pl.pallas_call(scatter_kernel, out_shape=jax.ShapeDtypeStruct((ROWS, HEAD...  24.7 us
    pallas_call x1, Pallas kernels, attend(): pl.pallas_call(attend_kernel, out_shape=(jax.ShapeDtypeStruct((2, GROUPS,...  12.6 us
    unnamed x12, local copies, waits for them, and re-layouts  3.52 us

profile of v1, /device:TPU:8, one launch (start us, length us, event | category | flops | bytes accessed | tf_op | source)
XLA Modules:
  0.0 95.1 jit_solution(636437536763892777)
XLA Ops:
  0.0 0.0 copy-start
  0.0 0.0 copy-start.1
  0.0 1.0 %copy-done.1 = bf16[1,24,4096]{2,1,0:T(8,128)(2,1)S(1)} copy-done((bf16[1,24,4096]{2,1,0:T(8,128)(2,1)S(1)}, bf16[1,24,4096]{2,1,0:T(8,128)(2,1)}, u32[]{:S(2)}) %copy-start.1) | copy-done | bytes 196632
  1.0 0.0 copy-start.2
  1.0 0.9 copy-done.2
  1.9 0.0 copy-start.3
  1.9 0.9 copy-done.3
  2.9 0.0 copy-start.5
  2.9 50.9 %gather.1 = (bf16[2,4,192,128]{3,2,1,0:T(8,128)(2,1)S(1)}, bf16[4,2,4,2,192,128]{5,4,3,2,1,0:T(8,128)(2,1)S(1)}) custom-call(bf16[1,24,4096]{2,1,0:T(8,128)(2,1)S(1)} %copy-done.1, bf16[1,24,4096]{2,1,0:T(8,128)(2,1)S(1)} %copy-done.2, bf16[1,24,4096]{2,1,0:T(8,128)(2,1)S(1)} %copy-done.3), custom_call_target="tpu_custom_call" | custom-call | tf_op jit(solution)/shard_map/gather/pallas_call | solution.py:193
  53.8 0.0 copy-start.4
  53.8 0.6 copy-done.4
  54.4 12.6 %attend.1 = (f32[2,4,192,128]{3,2,1,0:T(8,128)S(1)}, f32[2,4,8,128]{3,2,1,0:T(8,128)S(1)}) custom-call(s32[4]{0:T(128)S(1)} %copy-done.4, bf16[2,4,192,128]{3,2,1,0:T(8,128)(2,1)S(1)} %get-tuple-element.9.q_ref, bf16[4,2,1536,128]{3,2,1,0:T(8,128)(2,1)S(1)} %bitcast.5), custom_call_target="tpu_custom_call" | custom-call | tf_op jit(solution)/shard_map/attend/pallas_call | solution.py:267
  67.1 24.7 %scatter.1 = bf16[24,4096]{1,0:T(8,128)(2,1)S(1)} custom-call(f32[2,4,192,128]{3,2,1,0:T(8,128)S(1)} %get-tuple-element.11.o_ref, f32[2,4,8,128]{3,2,1,0:T(8,128)S(1)} %get-tuple-element.12.lse_ref), custom_call_target="tpu_custom_call" | custom-call | tf_op jit(solution)/shard_map/scatter/pallas_call | solution.py:340
  91.8 0.0 copy-done.5
  91.8 0.6 dynamic_slice.8
  94.4 0.0 copy-done
  94.4 0.7 fusion
  (1 shorter events, 0.0 us)
Async XLA Ops:
  0.0 94.4 %copy-start = (f32[50,4096]{1,0:T(8,128)S(1)}, f32[50,4096]{1,0:T(8,128)}, u32[]{:S(2)}) copy-start(f32[50,4096]{1,0:T(8,128)} %param.11) | copy-start | bytes 2457604
  0.0 1.0 %copy-start.1 = (bf16[1,24,4096]{2,1,0:T(8,128)(2,1)S(1)}, bf16[1,24,4096]{2,1,0:T(8,128)(2,1)}, u32[]{:S(2)}) copy-start(bf16[1,24,4096]{2,1,0:T(8,128)(2,1)} %q_ref.1) | copy-start | bytes 589828
  1.0 0.9 copy-start.2
  1.9 0.9 copy-start.3
  2.9 89.0 %copy-start.5 = (s32[4]{0:T(128)S(1)}, s32[4]{0:T(128)}, u32[]{:S(2)}) copy-start(s32[4]{0:T(128)} %param.9) | copy-start | bytes 52
  53.8 0.7 copy-start.4

commit v2 on v0

v2 whole, which is shorter than its diff:
```python
import jax
import jax.numpy as jnp
from jax import lax
from jax.experimental import pallas as pl
from jax.experimental.pallas import tpu as pltpu
from jax.sharding import PartitionSpec as P

HEADS = 32
HD = 128
GROUPS = 4
ROWS = 24
PAD = 32
SLOTS = 32
PART = 192
SUBSETS = 4
FOLD = HD**-0.5 * 1.4426950408889634
BF16, F32 = jnp.bfloat16, jnp.float32
MESH = pl.DeviceIdType.MESH


def rem(a, n):
    return lax.rem(a, jnp.int32(n))


class Place:
    def __init__(self):
        seq = lax.axis_index("seq")
        self.x = lax.axis_index("group")
        self.core = rem(seq, 2)
        self.y = rem(seq // 2, 8)
        self.z = seq // 16
        self.pair, self.j = self.y // 2, rem(self.y, 2)
        self.xs = [self.x] + [rem(self.x + i, 4) for i in range(1, 4)]
        self.zs = [self.z] + [rem(self.z + i, 8) for i in range(1, 8)]
        self.holders = []
        for r in range(4):
            pair = rem(self.pair + r, 4)
            e = rem(self.y - 2 * pair + 15, 8)
            j = 1 - e // 4
            slot = j * e + (1 - j) * (7 - e)
            self.holders.append((pair, (2 * pair + j) * 2 + self.core, slot))
        self.senders = [rem(self.y + (2 * self.j - 1) * slot + 8, 8) * 2 + self.core for slot in range(4)]

    def at(self, x, y, z, core):
        return {"group": x, "seq": z * 16 + y * 2 + core}

    def target(self, i):
        dz, r = i // 4, i % 4
        pair, low, slot = self.holders[r]
        z = self.zs[-dz % 8]
        return z * 4 + pair, dz * 4 + slot, z * 16 + low, self.xs[dz % 4]

    def source(self, i):
        dz, slot = i // 4, i % 4
        return self.zs[dz] * 16 + self.senders[slot], self.xs[-dz % 4]


def remote(src, dst, send, recv, device):
    return pltpu.make_async_remote_copy(src, dst, send, recv, device_id=device, device_id_type=MESH)


def landed(ref, sem):
    pltpu.make_async_copy(ref, ref, sem).wait()


def side_by_side(two):
    return jnp.concatenate([two[0].astype(F32), two[1].astype(F32)], axis=0).astype(BF16)


def diagonal():
    return lax.broadcasted_iota(jnp.int32, (64, HD), 0) == lax.broadcasted_iota(jnp.int32, (64, HD), 1)


def to_lanes(rows):
    return jnp.sum(jnp.where(diagonal(), rows, 0.0), axis=0, keepdims=True)


def to_column(lanes):
    return jnp.sum(jnp.where(diagonal(), lanes, 0.0), axis=1, keepdims=True)


def kernel(
    levels_ref, order_ref, q_hbm, k_hbm, v_hbm, gates_hbm, out_ref,
    q_ref, k_ref, v_ref, gates_ref, q_stage, kv_stage, q_got, kv_got, q_all, kv_0, kv_1, kv_2, kv_3, qq_ref, top_ref, total_ref,
    o_out, o_in, lse_out, lse_in, merged_ref, home_stage, home_got,
    load_sem, send_sem, q_sem, kv_sem, near_sem, far_sem, core_sem, pair_sem, o_sem, lse_sem, home_sem,
):
    me = Place()
    x, y, z, core = me.x, me.y, me.z, me.core
    right, left = me.at(me.xs[1], y, z, core), me.at(me.xs[3], y, z, core)
    other_core = me.at(x, y, z, 1 - core)
    partner = me.at(x, y + 1 - 2 * me.j, z, core)
    own = z * 4 + me.pair
    kv_all = kv_0, kv_1, kv_2, kv_3

    loads = [
        pltpu.make_async_copy(src, dst, load_sem.at[i])
        for i, (src, dst) in enumerate(((q_hbm.at[0], q_ref), (k_hbm.at[0], k_ref), (v_hbm.at[0], v_ref), (gates_hbm, gates_ref)))
    ]
    for copy in loads:
        copy.start()

    barrier = pltpu.get_barrier_semaphore()

    def greet(device):
        pl.semaphore_signal(barrier, inc=1, device_id=device, device_id_type=MESH)

    for i in range(1, SLOTS):
        seq, xq = me.source(i)
        greet({"group": x, "seq": seq})
        if (i // 4) % 4:
            greet({"group": xq, "seq": seq})
        _, _, seq, xq = me.target(i)
        greet({"group": xq, "seq": seq})
    for device in (right, left, other_core, partner):
        greet(device)

    for copy in loads:
        copy.wait()

    def stage(h, carry):
        columns = pl.ds(pl.multiple_of(h * HD, HD), HD)
        q_stage[h, :ROWS] = q_ref[:, columns]
        q_stage[h, ROWS:] = jnp.zeros((PAD - ROWS, HD), BF16)
        kv_stage[h] = side_by_side((k_ref[:, columns], v_ref[:, columns]))
        return carry

    lax.fori_loop(0, HEADS, stage, 0, unroll=4)
    q_got[0] = q_stage[own]
    kv_got[0] = kv_stage[own]
    pl.semaphore_wait(barrier, 31 + 24 + 31 + 4)

    for i in range(1, SLOTS):
        head, slot, seq, xq = me.target(i)
        remote(q_stage.at[head], q_got.at[slot], send_sem.at[0], q_sem, {"group": xq, "seq": seq}).start()
    for i in range(1, SLOTS):
        head, slot, seq, _ = me.target(i)
        remote(kv_stage.at[head], kv_got.at[slot], send_sem.at[1], kv_sem.at[i // 8], {"group": x, "seq": seq}).start()

    sent = []

    def push(src, dst, recv, device):
        copy = remote(src, dst, send_sem.at[3 + len(sent)], recv, device)
        copy.start()
        sent.append(copy)

    def part_of(group, t, which):
        return kv_all[t].at[group, :, which]

    def own_part(t):
        first = 1 if t == 0 else 0
        landed(kv_got.at[pl.ds(t * 8 + first, 8 - first)], kv_sem.at[t])
        for i in range(4):
            two = kv_got[t * 8 + 2 * i], kv_got[t * 8 + 2 * i + 1]
            rows = pl.ds(i * 48, 48)
            kv_all[t][x, 0, core, rows] = side_by_side((two[0][:ROWS], two[1][:ROWS]))
            kv_all[t][x, 1, core, rows] = side_by_side((two[0][ROWS:], two[1][ROWS:]))
        mine = part_of(x, t, core)
        push(mine, mine, near_sem.at[0, t], right)
        push(mine, mine, near_sem.at[1, t], left)
        push(mine, mine, core_sem.at[0, t], other_core)

    def forward(t):
        from_left, from_right = me.xs[3], me.xs[1]
        landed(part_of(from_left, t, core), near_sem.at[0, t])
        keys = kv_all[t].at[from_left, 0, core]
        push(keys, keys, far_sem.at[0, t], right)
        held = part_of(from_left, t, core)
        push(held, held, core_sem.at[1, t], other_core)
        landed(part_of(from_right, t, core), near_sem.at[1, t])
        values = kv_all[t].at[from_right, 1, core]
        push(values, values, far_sem.at[1, t], left)
        held = part_of(from_right, t, core)
        push(held, held, core_sem.at[2, t], other_core)

    def far(t):
        opposite = me.xs[2]
        landed(kv_all[t].at[opposite, 0, core], far_sem.at[0, t])
        landed(kv_all[t].at[opposite, 1, core], far_sem.at[1, t])
        held = part_of(opposite, t, core)
        push(held, held, core_sem.at[3, t], other_core)

    def arrive(t):
        for i, dx in enumerate((0, 3, 1, 2)):
            landed(part_of(me.xs[dx], t, 1 - core), core_sem.at[i, t])

    def queries():
        landed(q_got.at[pl.ds(1, SLOTS - 1)], q_sem)
        for dz in range(4):
            group = me.xs[-dz % 4]
            for i in range(4):
                slot = dz * 4 + (i // 2) * 16 + (i % 2) * 2
                q_all[me.j, group, pl.ds(i * 48, 48)] = side_by_side((q_got[slot, :ROWS], q_got[slot + 1, :ROWS]))
            push(q_all.at[me.j, group], q_all.at[me.j, group], pair_sem.at[dz], partner)

    def before(o, g):
        return (order_ref[o] <= order_ref[g] if o < g else order_ref[o] < order_ref[g]).astype(jnp.int32)

    ranks = [sum(before(o, g) for o in range(GROUPS) if o != g) for g in range(GROUPS)]
    at_rank = [sum(jnp.where(ranks[g] == r, g, 0) for g in range(GROUPS)) for r in range(GROUPS)]

    def queries_of_pair():
        for dz in range(4):
            landed(q_all.at[1 - me.j, me.xs[-dz % 4]], pair_sem.at[dz])
        for r in range(GROUPS):
            for i, j in enumerate((1 - me.j, me.j)):
                qq_ref[pl.ds((2 * r + i) * PART, PART)] = q_all[j, at_rank[r]]

    count = 2 * PART

    def scores_of(t, other):
        keys = kv_all[t][at_rank[other], 0].reshape(count, HD)
        queries = qq_ref[pl.ds(other * count, (GROUPS - other) * count)]
        return lax.dot_general(queries, keys, (((1,), (1,)), ((), ())), preferred_element_type=F32) * FOLD

    def add(t, other, scores):
        rows = pl.ds(other * count, (GROUPS - other) * count)
        values = jnp.concatenate([kv_all[t][at_rank[other], 1].reshape(count, HD), jnp.ones((count, HD), BF16)], axis=1)
        top = jnp.max(scores, axis=-1, keepdims=True)
        if t or other:
            before = top_ref[rows]
            now = jnp.maximum(before, top)
            weights = jnp.exp2(scores - now[:, :1]).astype(BF16)
            mixed = jnp.dot(weights, values, preferred_element_type=F32)
            shrink = jnp.exp2(before - now)
            total_ref[rows, :HD] = total_ref[rows, :HD] * shrink + mixed[:, :HD]
            total_ref[rows, HD:] = total_ref[rows, HD:] * shrink + mixed[:, HD:]
            top_ref[rows] = now
        else:
            weights = jnp.exp2(scores - top).astype(BF16)
            total_ref[rows] = jnp.dot(weights, values, preferred_element_type=F32)
            top_ref[rows] = jnp.broadcast_to(top, (scores.shape[0], HD))

    def attend(t):
        scores = scores_of(t, 0)
        for other in range(GROUPS):
            following = scores_of(t, other + 1) if other + 1 < GROUPS else None
            add(t, other, scores)
            scores = following

    own_part(0)
    queries()
    own_part(1)
    forward(0)
    own_part(2)
    forward(1)
    far(0)
    queries_of_pair()
    own_part(3)
    forward(2)
    far(1)
    arrive(0)
    attend(0)
    forward(3)
    far(2)
    arrive(1)
    attend(1)
    far(3)
    arrive(2)
    attend(2)
    arrive(3)
    attend(3)

    for r in range(GROUPS):
        rows = pl.ds(2 * r * PART, PART)
        sums = total_ref[rows, HD:]
        o_out[r] = (total_ref[rows, :HD] / sums).astype(BF16)
        lse = top_ref[rows] + jnp.log2(sums)
        lse_out[r] = jnp.concatenate([to_lanes(lse[i : i + 64]) for i in range(0, PART, 64)] + [jnp.zeros((5, HD), F32)], axis=0)
        push(lse_out.at[r], lse_in.at[r], lse_sem.at[r], partner)
        push(o_out.at[r], o_in.at[r], o_sem.at[r], partner)
    for r in range(GROUPS):
        rows = pl.ds((2 * r + 1) * PART, PART)
        sums = total_ref[rows, HD:]
        mine = total_ref[rows, :HD] / sums
        lse = top_ref[rows] + jnp.log2(sums)
        landed(lse_in.at[r], lse_sem.at[r])
        landed(o_in.at[r], o_sem.at[r])
        for i in range(3):
            theirs = o_in[r, pl.ds(i * 64, 64)].astype(F32)
            weight = 1.0 / (1.0 + jnp.exp2(to_column(lse_in[r, pl.ds(i, 1)]) - lse[i * 64 : i * 64 + 64]))
            merged_ref[r, pl.ds(i * 64, 64)] = theirs + (mine[i * 64 : i * 64 + 64] - theirs) * weight

    for dz in range(4):
        group = me.xs[-dz % 4]
        rank = sum(jnp.where(group == g, ranks[g], 0) for g in range(GROUPS))
        merged = merged_ref[rank].astype(F32)
        for i in range(8):
            slot = dz * 4 + (i // 4) * 16 + i % 4
            home_stage[slot, :ROWS] = merged[i * ROWS : i * ROWS + ROWS].astype(BF16)
            home_stage[slot, ROWS:] = jnp.zeros((PAD - ROWS, HD), BF16)
            if slot == 0:
                home_got[own] = home_stage[0]
            else:
                seq, xq = me.source(slot)
                remote(home_stage.at[slot], home_got.at[own], send_sem.at[2], home_sem, {"group": xq, "seq": seq}).start()

    level = levels_ref[x]
    gate = gates_ref[pl.ds(level, 1)]
    landed(home_got.at[pl.ds(1, SLOTS - 1)], home_sem)
    for h in range(HEADS):
        columns = slice(h * HD, h * HD + HD)
        out_ref[0, :, columns] = (home_got[h, :ROWS].astype(F32) * gate[:, columns]).astype(BF16)
    landed(q_stage.at[pl.ds(1, SLOTS - 1)], send_sem.at[0])
    landed(kv_stage.at[pl.ds(1, SLOTS - 1)], send_sem.at[1])
    landed(home_stage.at[pl.ds(1, SLOTS - 1)], send_sem.at[2])
    for copy in sent:
        copy.wait_send()


def shards(query_vectors, key_vectors, value_vectors, levels, causal_order, level_gates):
    vmem, dma = pltpu.VMEM, pltpu.SemaphoreType.DMA
    smem, anywhere = pl.BlockSpec(memory_space=pltpu.SMEM), pl.BlockSpec(memory_space=pl.ANY)
    wide = HEADS * HD
    return pl.pallas_call(
        kernel,
        out_shape=jax.ShapeDtypeStruct((1, ROWS, wide), BF16),
        in_specs=[smem, smem, anywhere, anywhere, anywhere, anywhere],
        out_specs=pl.BlockSpec(memory_space=vmem),
        scratch_shapes=[
            *[vmem((ROWS, wide), BF16)] * 3,
            vmem(level_gates.shape, F32),
            *[vmem((HEADS, PAD, HD), BF16), vmem((HEADS, 2 * ROWS, HD), BF16)] * 2,
            vmem((2, GROUPS, PART, HD), BF16),
            *[vmem((GROUPS, 2, 2, PART, HD), BF16)] * SUBSETS,
            vmem((2 * GROUPS * PART, HD), BF16),
            vmem((2 * GROUPS * PART, HD), F32),
            vmem((2 * GROUPS * PART, 2 * HD), F32),
            *[vmem((GROUPS, PART, HD), BF16)] * 2,
            *[vmem((GROUPS, 8, HD), F32)] * 2,
            vmem((GROUPS, PART, HD), F32),
            *[vmem((HEADS, PAD, HD), BF16)] * 2,
            dma((4,)), dma((64,)), dma, dma((SUBSETS,)), dma((2, SUBSETS)), dma((2, SUBSETS)), dma((4, SUBSETS)),
            dma((GROUPS,)), dma((GROUPS,)), dma((GROUPS,)), dma,
        ],
        compiler_params=pltpu.CompilerParams(collective_id=0, has_side_effects=True, vmem_limit_bytes=56 * 2**20),
        name="attention",
    )(levels, causal_order, query_vectors, key_vectors, value_vectors, level_gates)


def solution(mesh):
    placed = P("group", "seq", None)
    return jax.shard_map(
        shards, mesh=mesh, in_specs=(placed, placed, placed, P(), P(), P()), out_specs=placed, check_vma=False
    )
```

time: 222 us -> 71.4 us (0.32)
  the two profiles are of different devices: /device:TPU:5 before, /device:TPU:64 now
where the time goes in v2:
time: 71.4 us; the launch traced here: 71.2 us
  Pallas kernels  69.6 us (97%)
  local copies, waits for them, and re-layouts  1.62 us (2%)
    pallas_call x1, Pallas kernels, shards(): pl.pallas_call(kernel, out_shape=jax.ShapeDtypeStruct((1, ROWS, wide), BF...  69.6 us
    unnamed x1, local copies, waits for them, and re-layouts  1.62 us

profile of v2, /device:TPU:64, one launch (start us, length us, event | category | flops | bytes accessed | tf_op | source)
XLA Modules:
  0.0 71.2 jit_solution(14635762827915758624)
XLA Ops:
  0.0 69.6 %attention.1 = bf16[1,24,4096]{2,1,0:T(8,128)(2,1)} custom-call(s32[4]{0:T(128)} %levels_ref.1, s32[4]{0:T(128)} %order_ref.1, bf16[1,24,4096]{2,1,0:T(8,128)(2,1)} %q_hbm.1, bf16[1,24,4096]{2,1,0:T(8,128)(2,1)} %k_hbm.1, bf16[1,24,4096]{2,1,0:T(8,128)(2,1)} %v_hbm.1, f32[50,4096]{1,0:T(8,128)} %gates_hbm.1), custom_call_target="tpu_custom_call" | custom-call | tf_op jit(solution)/shard_map/attention/pallas_call | solution.py:315
  69.6 1.6 %copy.8 = bf16[1,24,4096]{2,1,0:T(8,128)(2,1)} copy(bf16[1,24,4096]{2,1,0:T(8,128)(2,1)} %attention.1) | data formatting | bytes 393216

commit v3 on v2

--- a/solution.py
+++ b/solution.py
@@ -13,6 +13,9 @@
 SLOTS = 32
 PART = 192
 SUBSETS = 4
+ORDER = (1, 7, 2, 6, 3, 5, 4, 0)
+SELF = 4 * ORDER.index(0)
+REMOTE = [i for i in range(SLOTS) if i != SELF]
 FOLD = HD**-0.5 * 1.4426950408889634
 BF16, F32 = jnp.bfloat16, jnp.float32
 MESH = pl.DeviceIdType.MESH
@@ -45,13 +48,13 @@
         return {"group": x, "seq": z * 16 + y * 2 + core}
 
     def target(self, i):
-        dz, r = i // 4, i % 4
+        dz, r = ORDER[i // 4], i % 4
         pair, low, slot = self.holders[r]
         z = self.zs[-dz % 8]
-        return z * 4 + pair, dz * 4 + slot, z * 16 + low, self.xs[dz % 4]
+        return z * 4 + pair, i // 4 * 4 + slot, z * 16 + low, self.xs[dz % 4]
 
     def source(self, i):
-        dz, slot = i // 4, i % 4
+        dz, slot = ORDER[i // 4], i % 4
         return self.zs[dz] * 16 + self.senders[slot], self.xs[-dz % 4]
 
 
@@ -80,7 +83,7 @@
 
 
 def kernel(
-    levels_ref, order_ref, q_hbm, k_hbm, v_hbm, gates_hbm, out_ref,
+    levels_ref, order_ref, q_hbm, k_hbm, v_hbm, gates_hbm, out_ref, gate_ref,
     q_ref, k_ref, v_ref, gates_ref, q_stage, kv_stage, q_got, kv_got, q_all, kv_0, kv_1, kv_2, kv_3, qq_ref, top_ref, total_ref,
     o_out, o_in, lse_out, lse_in, merged_ref, home_stage, home_got,
     load_sem, send_sem, q_sem, kv_sem, near_sem, far_sem, core_sem, pair_sem, o_sem, lse_sem, home_sem,
@@ -105,13 +108,11 @@
     def greet(device):
         pl.semaphore_signal(barrier, inc=1, device_id=device, device_id_type=MESH)
 
-    for i in range(1, SLOTS):
+    for i in reversed(REMOTE):
         seq, xq = me.source(i)
         greet({"group": x, "seq": seq})
-        if (i // 4) % 4:
+        if ORDER[i // 4] % 4:
             greet({"group": xq, "seq": seq})
-        _, _, seq, xq = me.target(i)
-        greet({"group": xq, "seq": seq})
     for device in (right, left, other_core, partner):
         greet(device)
 
@@ -126,57 +127,68 @@
         return carry
 
     lax.fori_loop(0, HEADS, stage, 0, unroll=4)
-    q_got[0] = q_stage[own]
-    kv_got[0] = kv_stage[own]
-    pl.semaphore_wait(barrier, 31 + 24 + 31 + 4)
-
-    for i in range(1, SLOTS):
-        head, slot, seq, xq = me.target(i)
-        remote(q_stage.at[head], q_got.at[slot], send_sem.at[0], q_sem, {"group": xq, "seq": seq}).start()
-    for i in range(1, SLOTS):
-        head, slot, seq, _ = me.target(i)
-        remote(kv_stage.at[head], kv_got.at[slot], send_sem.at[1], kv_sem.at[i // 8], {"group": x, "seq": seq}).start()
+    q_got[SELF] = q_stage[own]
+    kv_got[SELF] = kv_stage[own]
+    pl.semaphore_wait(barrier, 31 + 24 + 4)
+
+    def send_q():
+        for i in REMOTE:
+            head, slot, seq, xq = me.target(i)
+            remote(q_stage.at[head], q_got.at[slot], send_sem.at[0], q_sem, {"group": xq, "seq": seq}).start()
+
+    def send_kv(t):
+        for i in REMOTE:
+            if i // 8 == t:
+                head, slot, seq, _ = me.target(i)
+                remote(kv_stage.at[head], kv_got.at[slot], send_sem.at[1], kv_sem.at[t], {"group": x, "seq": seq}).start()
+
+    send_q()
+    send_kv(0)
+    send_kv(1)
+    send_kv(2)
+    send_kv(3)
 
     sent = []
 
-    def push(src, dst, recv, device):
-        copy = remote(src, dst, send_sem.at[3 + len(sent)], recv, device)
-        copy.start()
-        sent.append(copy)
+    def push(src, dst, recv, device, pieces=1):
+        sem, rows = send_sem.at[3 + len(sent)], src.shape[0] // pieces
+        for i in range(pieces):
+            piece = pl.ds(i * rows, rows)
+            remote(src.at[piece], dst.at[piece], sem, recv, device).start()
+        sent.append(remote(src, dst, sem, recv, device))
 
     def part_of(group, t, which):
-        return kv_all[t].at[group, :, which]
+        return kv_all[t].at[group, which]
 
     def own_part(t):
-        first = 1 if t == 0 else 0
-        landed(kv_got.at[pl.ds(t * 8 + first, 8 - first)], kv_sem.at[t])
+        landed(kv_got.at[pl.ds(t * 8, 7 if t == SELF // 8 else 8)], kv_sem.at[t])
         for i in range(4):
             two = kv_got[t * 8 + 2 * i], kv_got[t * 8 + 2 * i + 1]
             rows = pl.ds(i * 48, 48)
-            kv_all[t][x, 0, core, rows] = side_by_side((two[0][:ROWS], two[1][:ROWS]))
-            kv_all[t][x, 1, core, rows] = side_by_side((two[0][ROWS:], two[1][ROWS:]))
+            kv_all[t][x, core, 0, rows] = side_by_side((two[0][:ROWS], two[1][:ROWS]))
+            kv_all[t][x, core, 1, rows] = side_by_side((two[0][ROWS:], two[1][ROWS:]))
         mine = part_of(x, t, core)
+        push(mine, mine, core_sem.at[0, t], other_core)
         push(mine, mine, near_sem.at[0, t], right)
         push(mine, mine, near_sem.at[1, t], left)
-        push(mine, mine, core_sem.at[0, t], other_core)
 
     def forward(t):
         from_left, from_right = me.xs[3], me.xs[1]
         landed(part_of(from_left, t, core), near_sem.at[0, t])
-        keys = kv_all[t].at[from_left, 0, core]
-        push(keys, keys, far_sem.at[0, t], right)
         held = part_of(from_left, t, core)
         push(held, held, core_sem.at[1, t], other_core)
+        keys = kv_all[t].at[from_left, core, 0]
+        push(keys, keys, far_sem.at[0, t], right)
         landed(part_of(from_right, t, core), near_sem.at[1, t])
-        values = kv_all[t].at[from_right, 1, core]
-        push(values, values, far_sem.at[1, t], left)
         held = part_of(from_right, t, core)
         push(held, held, core_sem.at[2, t], other_core)
+        values = kv_all[t].at[from_right, core, 1]
+        push(values, values, far_sem.at[1, t], left)
 
     def far(t):
         opposite = me.xs[2]
-        landed(kv_all[t].at[opposite, 0, core], far_sem.at[0, t])
-        landed(kv_all[t].at[opposite, 1, core], far_sem.at[1, t])
+        landed(kv_all[t].at[opposite, core, 0], far_sem.at[0, t])
+        landed(kv_all[t].at[opposite, core, 1], far_sem.at[1, t])
         held = part_of(opposite, t, core)
         push(held, held, core_sem.at[3, t], other_core)
 
@@ -189,9 +201,9 @@
         for dz in range(4):
             group = me.xs[-dz % 4]
             for i in range(4):
-                slot = dz * 4 + (i // 2) * 16 + (i % 2) * 2
+                slot = 4 * ORDER.index(dz + i // 2 * 4) + i % 2 * 2
                 q_all[me.j, group, pl.ds(i * 48, 48)] = side_by_side((q_got[slot, :ROWS], q_got[slot + 1, :ROWS]))
-            push(q_all.at[me.j, group], q_all.at[me.j, group], pair_sem.at[dz], partner)
+            push(q_all.at[me.j, group], q_all.at[me.j, group], pair_sem.at[dz], partner, 4)
 
     def before(o, g):
         return (order_ref[o] <= order_ref[g] if o < g else order_ref[o] < order_ref[g]).astype(jnp.int32)
@@ -209,13 +221,13 @@
     count = 2 * PART
 
     def scores_of(t, other):
-        keys = kv_all[t][at_rank[other], 0].reshape(count, HD)
+        keys = kv_all[t][at_rank[other], :, 0].reshape(count, HD)
         queries = qq_ref[pl.ds(other * count, (GROUPS - other) * count)]
         return lax.dot_general(queries, keys, (((1,), (1,)), ((), ())), preferred_element_type=F32) * FOLD
 
     def add(t, other, scores):
         rows = pl.ds(other * count, (GROUPS - other) * count)
-        values = jnp.concatenate([kv_all[t][at_rank[other], 1].reshape(count, HD), jnp.ones((count, HD), BF16)], axis=1)
+        values = jnp.concatenate([kv_all[t][at_rank[other], :, 1].reshape(count, HD), jnp.ones((count, HD), BF16)], axis=1)
         top = jnp.max(scores, axis=-1, keepdims=True)
         if t or other:
             before = top_ref[rows]
@@ -231,11 +243,33 @@
             total_ref[rows] = jnp.dot(weights, values, preferred_element_type=F32)
             top_ref[rows] = jnp.broadcast_to(top, (scores.shape[0], HD))
 
-    def attend(t):
-        scores = scores_of(t, 0)
-        for other in range(GROUPS):
-            following = scores_of(t, other + 1) if other + 1 < GROUPS else None
+    def finish(r):
+        rows = pl.ds(2 * r * PART, PART)
+        sums = total_ref[rows, HD:]
+        o_out[r] = (total_ref[rows, :HD] / sums).astype(BF16)
+        lse = top_ref[rows] + jnp.log2(sums)
+        lse_out[r] = jnp.concatenate([to_lanes(lse[i : i + 64]) for i in range(0, PART, 64)] + [jnp.zeros((5, HD), F32)], axis=0)
+        push(lse_out.at[r], lse_in.at[r], lse_sem.at[r], partner)
+        push(o_out.at[r], o_in.at[r], o_sem.at[r], partner, 4)
+
+    def meanwhile(t):
+        if t == 0:
+            forward(3)
+            far(2)
+        if t == 1:
+            far(3)
+        arrive(t + 1)
+
+    def attend():
+        blocks = [(t, other) for t in range(SUBSETS) for other in range(GROUPS)]
+        scores = scores_of(0, 0)
+        for i, (t, other) in enumerate(blocks):
+            if other == GROUPS - 1 and t < SUBSETS - 1:
+                meanwhile(t)
+            following = scores_of(*blocks[i + 1]) if i + 1 < len(blocks) else None
             add(t, other, scores)
+            if t == SUBSETS - 1:
+                finish(other)
             scores = following
 
     own_part(0)
@@ -250,25 +284,8 @@
     forward(2)
     far(1)
     arrive(0)
-    attend(0)
-    forward(3)
-    far(2)
-    arrive(1)
-    attend(1)
-    far(3)
-    arrive(2)
-    attend(2)
-    arrive(3)
-    attend(3)
-
-    for r in range(GROUPS):
-        rows = pl.ds(2 * r * PART, PART)
-        sums = total_ref[rows, HD:]
-        o_out[r] = (total_ref[rows, :HD] / sums).astype(BF16)
-        lse = top_ref[rows] + jnp.log2(sums)
-        lse_out[r] = jnp.concatenate([to_lanes(lse[i : i + 64]) for i in range(0, PART, 64)] + [jnp.zeros((5, HD), F32)], axis=0)
-        push(lse_out.at[r], lse_in.at[r], lse_sem.at[r], partner)
-        push(o_out.at[r], o_in.at[r], o_sem.at[r], partner)
+    attend()
+
     for r in range(GROUPS):
         rows = pl.ds((2 * r + 1) * PART, PART)
         sums = total_ref[rows, HD:]
@@ -286,21 +303,20 @@
         rank = sum(jnp.where(group == g, ranks[g], 0) for g in range(GROUPS))
         merged = merged_ref[rank].astype(F32)
         for i in range(8):
-            slot = dz * 4 + (i // 4) * 16 + i % 4
+            slot = 4 * ORDER.index(dz + i // 4 * 4) + i % 4
             home_stage[slot, :ROWS] = merged[i * ROWS : i * ROWS + ROWS].astype(BF16)
             home_stage[slot, ROWS:] = jnp.zeros((PAD - ROWS, HD), BF16)
-            if slot == 0:
-                home_got[own] = home_stage[0]
+            if slot == SELF:
+                home_got[own] = home_stage[SELF]
             else:
                 seq, xq = me.source(slot)
                 remote(home_stage.at[slot], home_got.at[own], send_sem.at[2], home_sem, {"group": xq, "seq": seq}).start()
 
-    level = levels_ref[x]
-    gate = gates_ref[pl.ds(level, 1)]
+    gate_ref[...] = gates_ref[pl.ds(levels_ref[x], 1)]
     landed(home_got.at[pl.ds(1, SLOTS - 1)], home_sem)
     for h in range(HEADS):
         columns = slice(h * HD, h * HD + HD)
-        out_ref[0, :, columns] = (home_got[h, :ROWS].astype(F32) * gate[:, columns]).astype(BF16)
+        out_ref[:, columns] = home_got[h, :ROWS]
     landed(q_stage.at[pl.ds(1, SLOTS - 1)], send_sem.at[0])
     landed(kv_stage.at[pl.ds(1, SLOTS - 1)], send_sem.at[1])
     landed(home_stage.at[pl.ds(1, SLOTS - 1)], send_sem.at[2])
@@ -312,11 +328,11 @@
     vmem, dma = pltpu.VMEM, pltpu.SemaphoreType.DMA
     smem, anywhere = pl.BlockSpec(memory_space=pltpu.SMEM), pl.BlockSpec(memory_space=pl.ANY)
     wide = HEADS * HD
-    return pl.pallas_call(
+    joined, gate = pl.pallas_call(
         kernel,
-        out_shape=jax.ShapeDtypeStruct((1, ROWS, wide), BF16),
+        out_shape=(jax.ShapeDtypeStruct((ROWS, wide), BF16), jax.ShapeDtypeStruct((1, wide), F32)),
         in_specs=[smem, smem, anywhere, anywhere, anywhere, anywhere],
-        out_specs=pl.BlockSpec(memory_space=vmem),
+        out_specs=(pl.BlockSpec(memory_space=vmem), pl.BlockSpec(memory_space=vmem)),
         scratch_shapes=[
             *[vmem((ROWS, wide), BF16)] * 3,
             vmem(level_gates.shape, F32),
@@ -336,6 +352,7 @@
         compiler_params=pltpu.CompilerParams(collective_id=0, has_side_effects=True, vmem_limit_bytes=56 * 2**20),
         name="attention",
     )(levels, causal_order, query_vectors, key_vectors, value_vectors, level_gates)
+    return (joined.astype(F32) * gate).astype(BF16)[None]
 
 
 def solution(mesh):

time: 71.4 us -> 70.6 us (0.989)
  the two profiles are of different devices: /device:TPU:64 before, /device:TPU:2 now
where the time goes in v3:
time: 70.6 us; the launch traced here: 70.4 us
  Pallas kernels  68.7 us (97%)
  other arithmetic  1.64 us (2%)
    pallas_call x1, Pallas kernels, shards(): pl.pallas_call(kernel, out_shape=(jax.ShapeDtypeStruct((ROWS, wide), BF16...  68.7 us
    broadcast_in_dim x1, other arithmetic, shards(): return (joined.astype(F32) * gate).astype(BF16)[None]  1.64 us

profile of v3, /device:TPU:2, one launch (start us, length us, event | category | flops | bytes accessed | tf_op | source)
XLA Modules:
  0.0 70.4 jit_solution(4413760440419814510)
XLA Ops:
  0.0 68.7 %attention.1 = (bf16[24,4096]{1,0:T(8,128)(2,1)}, f32[1,4096]{1,0:T(1,128)}) custom-call(s32[4]{0:T(128)} %levels_ref.1, s32[4]{0:T(128)} %order_ref.1, bf16[1,24,4096]{2,1,0:T(8,128)(2,1)} %q_hbm.1, bf16[1,24,4096]{2,1,0:T(8,128)(2,1)} %k_hbm.1, bf16[1,24,4096]{2,1,0:T(8,128)(2,1)} %v_hbm.1, f32[50,4096]{1,0:T(8,128)} %gates_hbm.1), custom_call_target="tpu_custom_call" | custom-call | tf_op jit(solution)/shard_map/attention/pallas_call | solution.py:331
  68.7 1.6 %fusion = bf16[1,24,4096]{2,1,0:T(8,128)(2,1)} fusion(bf16[24,4096]{1,0:T(8,128)(2,1)} %get-tuple-element.7, f32[4096]{0:T(1024)} %bitcast.3), kind=kLoop, calls=%fused_computation.1 | loop fusion | flops 294912 | bytes 409600 | tf_op jit(solution)/shard_map/broadcast_in_dim | solution.py:355

commit v4 on v3

--- a/solution.py
+++ b/solution.py
@@ -12,8 +12,10 @@
 PAD = 32
 SLOTS = 32
 PART = 192
-SUBSETS = 4
-ORDER = (1, 7, 2, 6, 3, 5, 4, 0)
+SIZES = (8, 8, 8, 8)
+SUBSETS = len(SIZES)
+STARTS = [sum(SIZES[:t]) for t in range(SUBSETS)]
+ORDER = (0, 1, 7, 2, 6, 3, 5, 4)
 SELF = 4 * ORDER.index(0)
 REMOTE = [i for i in range(SLOTS) if i != SELF]
 FOLD = HD**-0.5 * 1.4426950408889634
@@ -138,7 +140,7 @@
 
     def send_kv(t):
         for i in REMOTE:
-            if i // 8 == t:
+            if STARTS[t] <= i < STARTS[t] + SIZES[t]:
                 head, slot, seq, _ = me.target(i)
                 remote(kv_stage.at[head], kv_got.at[slot], send_sem.at[1], kv_sem.at[t], {"group": x, "seq": seq}).start()
 
@@ -161,9 +163,10 @@
         return kv_all[t].at[group, which]
 
     def own_part(t):
-        landed(kv_got.at[pl.ds(t * 8, 7 if t == SELF // 8 else 8)], kv_sem.at[t])
-        for i in range(4):
-            two = kv_got[t * 8 + 2 * i], kv_got[t * 8 + 2 * i + 1]
+        first, size = STARTS[t], SIZES[t]
+        landed(kv_got.at[pl.ds(first, size - int(first <= SELF < first + size))], kv_sem.at[t])
+        for i in range(size // 2):
+            two = kv_got[first + 2 * i], kv_got[first + 2 * i + 1]
             rows = pl.ds(i * 48, 48)
             kv_all[t][x, core, 0, rows] = side_by_side((two[0][:ROWS], two[1][:ROWS]))
             kv_all[t][x, core, 1, rows] = side_by_side((two[0][ROWS:], two[1][ROWS:]))
@@ -221,13 +224,14 @@
     count = 2 * PART
 
     def scores_of(t, other):
-        keys = kv_all[t][at_rank[other], :, 0].reshape(count, HD)
+        keys = kv_all[t][at_rank[other], :, 0].reshape(2 * SIZES[t] * ROWS, HD)
         queries = qq_ref[pl.ds(other * count, (GROUPS - other) * count)]
         return lax.dot_general(queries, keys, (((1,), (1,)), ((), ())), preferred_element_type=F32) * FOLD
 
     def add(t, other, scores):
         rows = pl.ds(other * count, (GROUPS - other) * count)
-        values = jnp.concatenate([kv_all[t][at_rank[other], :, 1].reshape(count, HD), jnp.ones((count, HD), BF16)], axis=1)
+        values = kv_all[t][at_rank[other], :, 1].reshape(2 * SIZES[t] * ROWS, HD)
+        values = jnp.concatenate([values, jnp.ones(values.shape, BF16)], axis=1)
         top = jnp.max(scores, axis=-1, keepdims=True)
         if t or other:
             before = top_ref[rows]
@@ -252,20 +256,18 @@
         push(lse_out.at[r], lse_in.at[r], lse_sem.at[r], partner)
         push(o_out.at[r], o_in.at[r], o_sem.at[r], partner, 4)
 
-    def meanwhile(t):
-        if t == 0:
-            forward(3)
-            far(2)
-        if t == 1:
-            far(3)
-        arrive(t + 1)
+    MEANWHILE = {
+        (0, 3): ((forward, 3), (far, 2), (arrive, 1)),
+        (1, 3): ((far, 3), (arrive, 2)),
+        (2, 3): ((arrive, 3),),
+    }
 
     def attend():
         blocks = [(t, other) for t in range(SUBSETS) for other in range(GROUPS)]
         scores = scores_of(0, 0)
         for i, (t, other) in enumerate(blocks):
-            if other == GROUPS - 1 and t < SUBSETS - 1:
-                meanwhile(t)
+            for step, subset in MEANWHILE.get((t, other), ()):
+                step(subset)
             following = scores_of(*blocks[i + 1]) if i + 1 < len(blocks) else None
             add(t, other, scores)
             if t == SUBSETS - 1:
@@ -338,7 +340,7 @@
             vmem(level_gates.shape, F32),
             *[vmem((HEADS, PAD, HD), BF16), vmem((HEADS, 2 * ROWS, HD), BF16)] * 2,
             vmem((2, GROUPS, PART, HD), BF16),
-            *[vmem((GROUPS, 2, 2, PART, HD), BF16)] * SUBSETS,
+            *[vmem((GROUPS, 2, 2, size * ROWS, HD), BF16) for size in SIZES],
             vmem((2 * GROUPS * PART, HD), BF16),
             vmem((2 * GROUPS * PART, HD), F32),
             vmem((2 * GROUPS * PART, 2 * HD), F32),

time: 70.6 us -> 70.2 us (level)
  no operation moved by 1% of the time
where the time goes in v4:
time: 70.2 us; the launch traced here: 70 us
  Pallas kernels  68.3 us (97%)
  other arithmetic  1.64 us (2%)
    pallas_call x1, Pallas kernels, shards(): pl.pallas_call(kernel, out_shape=(jax.ShapeDtypeStruct((ROWS, wide), BF16...  68.3 us
    broadcast_in_dim x1, other arithmetic, shards(): return (joined.astype(F32) * gate).astype(BF16)[None]  1.64 us

profile of v4, /device:TPU:2, one launch (start us, length us, event | category | flops | bytes accessed | tf_op | source)
XLA Modules:
  0.0 70.0 jit_solution(13808537327011133893)
XLA Ops:
  0.0 68.3 %attention.1 = (bf16[24,4096]{1,0:T(8,128)(2,1)}, f32[1,4096]{1,0:T(1,128)}) custom-call(s32[4]{0:T(128)} %levels_ref.1, s32[4]{0:T(128)} %order_ref.1, bf16[1,24,4096]{2,1,0:T(8,128)(2,1)} %q_hbm.1, bf16[1,24,4096]{2,1,0:T(8,128)(2,1)} %k_hbm.1, bf16[1,24,4096]{2,1,0:T(8,128)(2,1)} %v_hbm.1, f32[50,4096]{1,0:T(8,128)} %gates_hbm.1), custom_call_target="tpu_custom_call" | custom-call | tf_op jit(solution)/shard_map/attention/pallas_call | solution.py:333
  68.3 1.6 %fusion = bf16[1,24,4096]{2,1,0:T(8,128)(2,1)} fusion(bf16[24,4096]{1,0:T(8,128)(2,1)} %get-tuple-element.7, f32[4096]{0:T(1024)} %bitcast.3), kind=kLoop, calls=%fused_computation.1 | loop fusion | flops 294912 | bytes 409600 | tf_op jit(solution)/shard_map/broadcast_in_dim | solution.py:357
